TPU v7x, 32 devices: a whole 2x2x4 slice. The times are simulated.
32 devices in a mesh: gx: 4 (over y, core), gy: 4 (over z), pa: 2 (over x).
Axes of the slice: x: 2, y: 2, z: 4, core: 2. Of those that a mesh axis runs over, the one named last changes fastest.
Arguments:
- volume: bfloat16 [4, 2048, 1024], P('pa', 'gx', 'gy'), may hold values from -6 to 6
- view_slopes: int32 [2, 16], replicated, may hold values from -14 to 14, as said below
- measured_x: float32 [16, 4, 1024], P(None, 'pa', 'gy'), may hold values from -6 to 6
- measured_y: float32 [16, 4, 2048], P(None, 'pa', 'gx'), may hold values from -6 to 6
Outputs:
- gradient: float32 [4, 2048, 1024], P('pa', 'gx', 'gy')
- residual_x: float32 [16, 4, 1024], P(None, 'pa', 'gy')
- residual_y: float32 [16, 4, 2048], P(None, 'pa', 'gx')
Inputs may be any that keep to these rules, and one draw needn't show every extreme that they name: `view_slopes`: row 0 holds the near-x slopes in units of 1/512, row 1 the near-y slopes in units of 1/256; in each row both 14 and its negative occur.
All inputs are finite; a program needn't handle non-finite values.
Results may differ from a plain program's by a relative error of at most 0.0025.
Values may be sent and summed in bfloat16 or wider, within the bound.
A program may use at most 128 MiB of HBM per device.

v0:
```python
import jax
import jax.numpy as jnp
from jax import lax
from jax.sharding import PartitionSpec as P

SHEAR = 14


def padded_2(value, sides, width):
    for axis, dim in sides:
        size, length = (lax.axis_size(axis), value.shape[dim])
        up = [(i, (i + 1) % size) for i in range(size - 1)]
        down = [(j, i) for i, j in up]
        last = lax.slice_in_dim(value, length - width, length, axis=dim)
        leading = lax.slice_in_dim(value, 0, width, axis=dim)
        before = lax.ppermute(last, axis, up)
        after = lax.ppermute(leading, axis, down)
        value = jnp.concatenate([before, value, after], axis=dim)
    return value


def lane_round(value):
    return -(-value // 128) * 128


def shear_table(slopes, positions, cells, shift_levels):
    product = slopes[:, None] * positions[None, :]
    shifts = jnp.floor_divide(product, cells)
    fraction = (product - shifts * cells).astype(jnp.float32) / cells
    lowest = jnp.min(shifts, axis=1)
    offsets = shifts - lowest[:, None]
    levels = jnp.arange(shift_levels, dtype=jnp.int32)
    lower = (1.0 - fraction).astype(jnp.bfloat16)
    upper = fraction.astype(jnp.bfloat16)
    nothing = jnp.zeros((), jnp.bfloat16)
    table = jnp.where(levels[None, :, None] == offsets[:, None, :], lower[:, None, :], nothing)
    table = table + jnp.where(
        levels[None, :, None] == offsets[:, None, :] + 1, upper[:, None, :], nothing
    )
    return (table, lowest)


def shear_sum(summands, lowest, leading, number, pad_cells):
    planes, shift_levels, length = summands.shape
    natural_row = length + 2 * pad_cells
    right_pad = pad_cells + lane_round(natural_row + 1) - (natural_row + 1)
    row_length = length + pad_cells + right_pad
    padded = jnp.pad(summands, ((0, 0), (0, 0), (pad_cells, right_pad)))
    flattened = jnp.pad(
        padded.reshape(planes, shift_levels * row_length), ((0, 0), (0, shift_levels))
    )
    skewed = jnp.sum(flattened.reshape(planes, shift_levels, row_length + 1), axis=1)
    return lax.dynamic_slice_in_dim(skewed, leading + lowest + pad_cells, number, 1)


def spread(values, lowest, leading, number, pad_cells, shift_levels):
    planes, length = values.shape
    natural_row = length + 2 * pad_cells
    right_pad = pad_cells + lane_round(natural_row - 1) - (natural_row - 1)
    row_length = length + pad_cells + right_pad
    padded = jnp.pad(values, ((0, 0), (pad_cells, right_pad)))
    repeated = jnp.broadcast_to(padded[:, None, :], (planes, shift_levels, row_length))
    repeated = repeated.reshape(planes, shift_levels * row_length)
    skewed = repeated[:, : shift_levels * (row_length - 1)].reshape(
        planes, shift_levels, row_length - 1
    )
    return lax.dynamic_slice_in_dim(skewed, leading - lowest + pad_cells, number, 2)


def sheared_views(summands, lowest, leading, number, pad_cells):
    return jax.vmap(lambda pieces, low: shear_sum(pieces, low, leading, number, pad_cells))(
        summands, lowest
    )


def spread_views(values, lowest, leading, number, pad_cells, shift_levels):
    return jax.vmap(
        lambda pieces, low: spread(pieces, low, leading, number, pad_cells, shift_levels)
    )(values, lowest)


def fold_edges(inner, outer, ghost_width, length, dim):
    lead_pads = [(0, 0)] * inner.ndim
    tail_pads = [(0, 0)] * inner.ndim
    lead_pads[dim] = (0, length - ghost_width)
    tail_pads[dim] = (length - ghost_width, 0)
    head = lax.slice_in_dim(outer, 0, ghost_width, 1, dim)
    tail = lax.slice_in_dim(outer, length + 3 * ghost_width, length + 4 * ghost_width, 1, dim)
    return inner + jnp.pad(head, lead_pads) + jnp.pad(tail, tail_pads)


def on_device(volume, view_slopes, measured_x, measured_y):
    planes, cells_x, cells_y = volume.shape
    count_x = lax.axis_size("gx")
    count_y = lax.axis_size("gy")
    ghost_width = SHEAR * max(count_x, count_y) // 2 + 2
    shift_levels = SHEAR + 2
    pad_cells = 2 * ghost_width + shift_levels
    positions_x = (
        lax.axis_index("gx") * cells_x
        + jnp.arange(cells_x, dtype=jnp.int32)
        - cells_x * count_x // 2
    )
    positions_y = (
        lax.axis_index("gy") * cells_y
        + jnp.arange(cells_y, dtype=jnp.int32)
        - cells_y * count_y // 2
    )
    table_x, lowest_x = shear_table(view_slopes[0], positions_x, cells_x, shift_levels)
    table_y, lowest_y = shear_table(view_slopes[1], positions_y, cells_y, shift_levels)
    scale_x = float(cells_x * count_x) ** (-0.5)
    scale_y = float(cells_y * count_y) ** (-0.5)
    layered = padded_2(volume, (("pa", 0),), 1).astype(jnp.float32)
    coupling = 0.02 * (2.0 * layered[1:-1] - layered[:-2] - layered[2:])
    leading = -ghost_width
    number_x = cells_y + 2 * ghost_width
    number_y = cells_x + 2 * ghost_width
    summands_x = jnp.einsum("vsx,pxy->vpsy", table_x, volume, preferred_element_type=jnp.float32)
    summands_x = sheared_views(summands_x, lowest_x, leading, number_x, pad_cells)
    summands_y = jnp.einsum("vsy,pxy->vpsx", table_y, volume, preferred_element_type=jnp.float32)
    summands_y = sheared_views(summands_y, lowest_y, leading, number_y, pad_cells)
    total_x = lax.psum(summands_x, "gx")
    total_y = lax.psum(summands_y, "gy")
    outer_x = padded_2(total_x.astype(jnp.bfloat16), (("gy", 2),), ghost_width).astype(
        total_x.dtype
    )
    own_x = fold_edges(
        total_x[:, :, ghost_width : ghost_width + cells_y], outer_x, ghost_width, cells_y, 2
    )
    outer_y = padded_2(total_y.astype(jnp.bfloat16), (("gx", 2),), ghost_width).astype(
        total_y.dtype
    )
    own_y = fold_edges(
        total_y[:, :, ghost_width : ghost_width + cells_x], outer_y, ghost_width, cells_x, 2
    )
    residual_x = own_x * scale_x - measured_x
    residual_y = own_y * scale_y - measured_y
    back_rx = residual_x.astype(jnp.bfloat16)
    back_ry = residual_y.astype(jnp.bfloat16)
    bins_x = padded_2(back_rx, (("gy", 2),), ghost_width)
    bins_y = padded_2(back_ry, (("gx", 2),), ghost_width)
    spread_x = spread_views(bins_x, lowest_x, ghost_width, cells_y, pad_cells, shift_levels)
    spread_y = spread_views(bins_y, lowest_y, ghost_width, cells_x, pad_cells, shift_levels)
    local_x = jnp.einsum("vsx,vpsy->pxy", table_x, spread_x, preferred_element_type=jnp.float32)
    local_y = jnp.einsum("vsy,vpsx->pxy", table_y, spread_y, preferred_element_type=jnp.float32)
    gradient = local_x * scale_x + local_y * scale_y + coupling
    return (gradient, residual_x, residual_y)


def solution(mesh):
    return jax.shard_map(
        on_device,
        mesh=mesh,
        in_specs=(P("pa", "gx", "gy"), P(), P(None, "pa", "gy"), P(None, "pa", "gx")),
        out_specs=(P("pa", "gx", "gy"), P(None, "pa", "gy"), P(None, "pa", "gx")),
        check_vma=False,
    )
```

profile of v0, /device:TPU:27, one launch (start us, length us, event | category | flops | bytes accessed | tf_op | source)
XLA Modules:
  0.0 160.8 jit_solution(13689655971994652050)
XLA Ops:
  7.2 0.8 slice_bitcast_fusion
  8.0 0.2 fusion.55
  8.2 0.1 subtract_convert_fusion.1
  8.3 0.1 broadcast_subtract_fusion.1
  8.4 0.6 copy-done.3
  9.0 1.4 convolution_bitcast_fusion.1
  10.4 0.4 pad.49
  10.8 2.1 %reshape.412 = f32[16,2,12272]{2,1,0:T(2,128)S(1)} reshape(f32[16,2,16,767]{3,2,1,0:T(8,128)S(1)} %pad.49) | data formatting | bytes 3141632 | tf_op jit(solution)/shard_map/vmap()/reshape | solution.py:50
  12.9 1.8 %pad.50 = f32[16,2,12288]{2,1,0:T(2,128)} pad(f32[16,2,12272]{2,1,0:T(2,128)S(1)} %reshape.412, f32[]{:T(128)} %constant.85.clone.1), padding=0_0x0_0x0_16 | pad | bytes 3143684 | tf_op jit(solution)/shard_map/vmap(jit(_pad))/pad | solution.py:49
  14.7 2.6 %reshape.413 = f32[16,2,16,768]{3,2,1,0:T(8,128)S(1)} reshape(f32[16,2,12288]{2,1,0:T(2,128)} %pad.50) | data formatting | bytes 3145728 | tf_op jit(solution)/shard_map/vmap()/reshape | solution.py:52
  17.3 0.3 reduce_sum.19
  17.6 4.8 %copy.83 = f32[16,2,768]{1,0,2:T(8,128)} copy(f32[16,2,768]{2,1,0:T(2,128)S(1)} %reduce_sum.19) | data formatting | bytes 196608 | tf_op jit(solution)/shard_map/vmap()/reduce_sum | solution.py:52
  22.4 8.5 %gather_fusion.2 = f32[16,2,572]{1,0,2:T(8,128)} fusion(f32[16,2,768]{1,0,2:T(8,128)} %copy.83, s32[16]{0:T(128)S(1)} %get-tuple-element.40), kind=kCustom, calls=%fused_computation.2 | custom fusion | bytes 146624 | tf_op jit(solution)/shard_map/vmap()/gather | solution.py:53
  30.9 3.8 %copy.84 = f32[16,2,572]{2,0,1:T(8,128)} copy(f32[16,2,572]{1,0,2:T(8,128)} %gather_fusion.2) | data formatting | bytes 146432 | tf_op jit(solution)/shard_map/vmap()/gather | solution.py:53
  34.8 0.2 fusion.52
  35.0 0.1 subtract_convert_fusion
  35.2 0.1 broadcast_subtract_fusion
  35.3 0.1 fusion.11
  35.4 0.3 convolution_bitcast_fusion.3
  35.7 0.3 pad.44
  36.0 1.4 reshape.408
  37.4 0.5 pad.45
  37.9 0.9 reshape.409
  38.9 0.2 reduce_sum.18
  39.1 3.4 %copy.77 = f32[16,2,512]{1,0,2:T(8,128)} copy(f32[16,2,512]{2,1,0:T(2,128)S(1)} %reduce_sum.18) | data formatting | bytes 131072 | tf_op jit(solution)/shard_map/vmap()/reduce_sum | solution.py:52
  42.6 4.5 %gather_fusion = f32[16,2,316]{1,0,2:T(8,128)S(1)} fusion(f32[16,2,512]{1,0,2:T(8,128)} %copy.77, s32[16]{0:T(128)S(1)} %get-tuple-element.42), kind=kCustom, calls=%fused_computation | custom fusion | bytes 81088 | tf_op jit(solution)/shard_map/vmap()/gather | solution.py:53
  47.1 1.3 copy.78
  48.5 10.7 %psum.14 = f32[16,2,316]{2,0,1:T(8,128)S(1)} all-reduce(f32[16,2,316]{2,0,1:T(8,128)S(1)} %copy.78), channel_id=1, replica_groups=mesh['gx'=4,'gy'=4,'pa'=2] {'gx'}, use_global_device_ids=true, to_apply=%region_2.3 | all-reduce | flops 10112 | bytes 80896 | tf_op jit(solution)/shard_map/psum | solution.py:122
  59.2 1.3 collective-permute-start
  60.5 4.0 %collective-permute-start.1 = (bf16[16,2,30]{2,0,1:T(8,128)(2,1)S(1)}, bf16[16,2,30]{2,0,1:T(8,128)(2,1)S(1)}, u32[]{:S(2)}, u32[]{:S(2)}) collective-permute-start(bf16[16,2,30]{2,0,1:T(8,128)(2,1)S(1)} %get-tuple-element.26), channel_id=1, source_target_pairs={{2,0},{4,2},{6,4},{3,1},{5,3},{7,5},{10,8},{12,10},{14,12},{11,9},... | collective-permute-start | bytes 5768 | tf_op jit(solution)/shard_map/ppermute | solution.py:17
  64.5 0.2 copy.89
  64.7 0.8 fusion.66
  65.6 1.3 collective-permute-start.8
  66.9 4.7 %collective-permute-start.9 = (bf16[1,512,256]{1,2,0:T(8,128)(2,1)}, bf16[1,512,256]{1,2,0:T(8,128)(2,1)}, u32[]{:S(2)}, u32[]{:S(2)}) collective-permute-start(bf16[1,512,256]{1,2,0:T(8,128)(2,1)} %get-tuple-element.20), channel_id=1, source_target_pairs={{1,0},{3,2},{5,4},{7,6},{9,8},{11,10},{13,12},{15,14},{17,16},{19,... | collective-permute-start | bytes 786440 | tf_op jit(solution)/shard_map/ppermute | solution.py:17
  71.9 1.3 collective-permute-start.2
  73.2 4.0 %collective-permute-start.3 = (bf16[16,2,30]{2,0,1:T(8,128)(2,1)S(1)}, bf16[16,2,30]{2,0,1:T(8,128)(2,1)S(1)}, u32[]{:S(2)}, u32[]{:S(2)}) collective-permute-start(bf16[16,2,30]{2,0,1:T(8,128)(2,1)S(1)} %get-tuple-element.28), channel_id=1, source_target_pairs={{2,0},{4,2},{6,4},{3,1},{5,3},{7,5},{10,8},{12,10},{14,12},{11,9},... | collective-permute-start | bytes 5768 | tf_op jit(solution)/shard_map/ppermute | solution.py:17
  77.2 0.6 copy.93
  77.8 0.9 convert_element_type.98
  78.7 0.7 fusion.67
  79.4 5.4 %collective-permute-start.4 = (bf16[16,2,30]{2,0,1:T(8,128)(2,1)}, bf16[16,2,30]{2,0,1:T(8,128)(2,1)}, u32[]{:S(2)}, u32[]{:S(2)}) collective-permute-start(bf16[16,2,30]{2,0,1:T(8,128)(2,1)} %get-tuple-element.21), channel_id=1, source_target_pairs={{0,8},{8,16},{16,24},{1,9},{9,17},{17,25},{2,10},{10,18},{18,26},{... | collective-permute-start | bytes 5768 | tf_op jit(solution)/shard_map/ppermute | solution.py:16
  84.8 1.9 %collective-permute-start.5 = (bf16[16,2,30]{2,0,1:T(8,128)(2,1)}, bf16[16,2,30]{2,0,1:T(8,128)(2,1)}, u32[]{:S(2)}, u32[]{:S(2)}) collective-permute-start(bf16[16,2,30]{2,0,1:T(8,128)(2,1)} %get-tuple-element.22), channel_id=1, source_target_pairs={{8,0},{16,8},{24,16},{9,1},{17,9},{25,17},{10,2},{18,10},{26,18},{... | collective-permute-start | bytes 5768 | tf_op jit(solution)/shard_map/ppermute | solution.py:17
  86.7 0.1 fusion.33
  86.9 0.6 reshape.410
  87.6 0.2 copy.104
  87.7 7.6 %copy.80 = bf16[16,2,16,512]{2,1,0,3:T(2,128)(2,1)} copy(bf16[16,2,16,512]{3,2,0,1:T(8,128)(2,1)S(1)} %bitcast.106) | data formatting | bytes 1048576 | tf_op jit(solution)/shard_map/vmap()/reshape | solution.py:64
  95.3 8.8 %gather_fusion.1 = bf16[16,2,16,256]{2,1,3,0:T(2,128)(2,1)S(1)} fusion(bf16[16,2,16,512]{2,1,0,3:T(2,128)(2,1)} %copy.80, s32[16]{0:T(128)S(1)} %get-tuple-element.41), kind=kCustom, calls=%fused_computation.1 | custom fusion | bytes 524544 | tf_op jit(solution)/shard_map/vmap()/gather | solution.py:67
  104.2 1.2 copy.81
  105.3 0.8 maximum_convert_fusion.1
  106.1 0.8 maximum_convert_fusion.3
  106.9 0.9 fusion.62
  107.9 3.6 %collective-permute-start.6 = (bf16[16,2,30]{2,0,1:T(8,128)(2,1)S(1)}, bf16[16,2,30]{2,0,1:T(8,128)(2,1)S(1)}, u32[]{:S(2)}, u32[]{:S(2)}) collective-permute-start(bf16[16,2,30]{2,0,1:T(8,128)(2,1)S(1)} %get-tuple-element.23), channel_id=1, source_target_pairs={{0,8},{8,16},{16,24},{1,9},{9,17},{17,25},{2,10},{10,18},{18,26},{... | collective-permute-start | bytes 5768 | tf_op jit(solution)/shard_map/ppermute | solution.py:16
  111.6 1.9 %collective-permute-start.7 = (bf16[16,2,30]{2,0,1:T(8,128)(2,1)S(1)}, bf16[16,2,30]{2,0,1:T(8,128)(2,1)S(1)}, u32[]{:S(2)}, u32[]{:S(2)}) collective-permute-start(bf16[16,2,30]{2,0,1:T(8,128)(2,1)S(1)} %get-tuple-element.24), channel_id=1, source_target_pairs={{8,0},{16,8},{24,16},{9,1},{17,9},{25,17},{10,2},{18,10},{26,18},{... | collective-permute-start | bytes 5768 | tf_op jit(solution)/shard_map/ppermute | solution.py:17
  113.5 2.1 %fusion.1 = f32[2,512,256]{1,2,0:T(8,128)} fusion(bf16[16,2,16,256]{3,0,2,1:T(8,128)(2,1)S(1)} %copy.81, s32[16,512]{1,0:T(8,128)} %copy-done.6, s32[16,512]{1,0:T(8,128)} %copy-done.5, bf16[16,512]{1,0:T(8,128)(2,1)} %copy-done.12, bf16[16,512]{1,0:T(8,128)(2,1)} %copy-done.11), kind=kOutput, calls=%fused_computation.8 | convolution fusion | flops 135528448 | bytes 1409024 | tf_op jit(solution)/shard_map/vsx,vpsy->pxy/dot_general | solution.py:144
  115.6 0.7 copy.94
  116.3 0.2 collective-permute-done.7
  116.5 0.1 fusion.28
  116.7 0.9 reshape.414
  117.7 0.1 copy.105
  117.8 11.5 %copy.86 = bf16[16,2,16,768]{2,1,0,3:T(2,128)(2,1)} copy(bf16[16,2,16,768]{3,2,0,1:T(8,128)(2,1)S(1)} %bitcast.104) | data formatting | bytes 1572864 | tf_op jit(solution)/shard_map/vmap()/reshape | solution.py:64
  129.3 15.5 %gather_fusion.3 = bf16[16,2,16,512]{2,1,3,0:T(2,128)(2,1)} fusion(bf16[16,2,16,768]{2,1,0,3:T(2,128)(2,1)} %copy.86, s32[16]{0:T(128)S(1)} %get-tuple-element.39), kind=kCustom, calls=%fused_computation.3 | custom fusion | bytes 1048832 | tf_op jit(solution)/shard_map/vmap()/gather | solution.py:67
  144.9 6.2 %copy.87 = bf16[16,2,16,512]{3,0,2,1:T(8,128)(2,1)S(1)} copy(bf16[16,2,16,512]{2,1,3,0:T(2,128)(2,1)} %gather_fusion.3) | data formatting | bytes 1048576 | tf_op jit(solution)/shard_map/vmap()/gather | solution.py:67
  151.1 1.1 maximum_convert_fusion
  152.2 0.4 fusion.4
  152.7 1.3 copy.92
  (57 shorter events, 0.9 us)
Async XLA Ops:
  7.2 70.7 %all-reduce.14.cloned.1.call-start = ((), (), s32[]{:S(2)}) async-start(), calls=%async_computation | async-start | bytes 163840 | tf_op jit(solution)/shard_map/psum | solution.py:123
  8.3 6.4 %copy-start.7 = (bf16[16,256]{1,0:T(8,128)(2,1)}, bf16[16,256]{1,0:T(8,128)(2,1)S(1)}, u32[]{:S(2)}) copy-start(bf16[16,256]{1,0:T(8,128)(2,1)S(1)} %get-tuple-element.35) | copy-start | bytes 24580
  8.3 6.4 %copy-start.9 = (bf16[16,256]{1,0:T(8,128)(2,1)}, bf16[16,256]{1,0:T(8,128)(2,1)S(1)}, u32[]{:S(2)}) copy-start(bf16[16,256]{1,0:T(8,128)(2,1)S(1)} %get-tuple-element.36) | copy-start | bytes 24580
  8.4 0.6 copy-start.3
  22.4 13.0 %copy-start = (bf16[2,512,256]{2,1,0:T(8,128)(2,1)S(1)}, bf16[2,512,256]{2,1,0:T(8,128)(2,1)}, u32[]{:S(2)}) copy-start(bf16[2,512,256]{2,1,0:T(8,128)(2,1)} %param.4) | copy-start | bytes 1572868
  35.1 3.7 %copy-start.11 = (bf16[16,512]{1,0:T(8,128)(2,1)}, bf16[16,512]{1,0:T(8,128)(2,1)S(1)}, u32[]{:S(2)}) copy-start(bf16[16,512]{1,0:T(8,128)(2,1)S(1)} %get-tuple-element.31) | copy-start | bytes 49156
  35.1 3.7 %copy-start.12 = (bf16[16,512]{1,0:T(8,128)(2,1)}, bf16[16,512]{1,0:T(8,128)(2,1)S(1)}, u32[]{:S(2)}) copy-start(bf16[16,512]{1,0:T(8,128)(2,1)S(1)} %get-tuple-element.32) | copy-start | bytes 49156
  35.3 3.6 %copy-start.5 = (s32[16,512]{1,0:T(8,128)}, s32[16,512]{1,0:T(8,128)S(1)}, u32[]{:S(2)}) copy-start(s32[16,512]{1,0:T(8,128)S(1)} %get-tuple-element.29) | copy-start | bytes 98308
  35.3 3.6 %copy-start.6 = (s32[16,512]{1,0:T(8,128)}, s32[16,512]{1,0:T(8,128)S(1)}, u32[]{:S(2)}) copy-start(s32[16,512]{1,0:T(8,128)S(1)} %get-tuple-element.30) | copy-start | bytes 98308
  39.1 32.6 %copy-start.13 = (f32[16,2,256]{2,1,0:T(2,128)S(1)}, f32[16,2,256]{2,1,0:T(2,128)}, u32[]{:S(2)}) copy-start(f32[16,2,256]{2,1,0:T(2,128)} %param.6) | copy-start | bytes 98308
  39.1 32.6 %copy-start.14 = (pred[256]{0:T(512)(128)(4,1)S(1)}, pred[256]{0:T(512)(128)(4,1)}, u32[]{:S(2)}) copy-start(pred[256]{0:T(512)(128)(4,1)} %constant.88.clone.1) | copy-start | bytes 772
  59.2 12.3 %collective-permute-start = (bf16[16,2,30]{2,0,1:T(8,128)(2,1)S(1)}, bf16[16,2,30]{2,0,1:T(8,128)(2,1)S(1)}, u32[]{:S(2)}, u32[]{:S(2)}) collective-permute-start(bf16[16,2,30]{2,0,1:T(8,128)(2,1)S(1)} %get-tuple-element.25), channel_id=1, source_target_pairs={{0,2},{2,4},{4,6},{1,3},{3,5},{5,7},{8,10},{10,12},{12,14},{9,11},... | collective-permute-start | bytes 5768 | tf_op jit(solution)/shard_map/ppermute | solution.py:16
  60.5 11.1 %collective-permute-start.1 = (bf16[16,2,30]{2,0,1:T(8,128)(2,1)S(1)}, bf16[16,2,30]{2,0,1:T(8,128)(2,1)S(1)}, u32[]{:S(2)}, u32[]{:S(2)}) collective-permute-start(bf16[16,2,30]{2,0,1:T(8,128)(2,1)S(1)} %get-tuple-element.26), channel_id=1, source_target_pairs={{2,0},{4,2},{6,4},{3,1},{5,3},{7,5},{10,8},{12,10},{14,12},{11,9},... | collective-permute-start | bytes 5768 | tf_op jit(solution)/shard_map/ppermute | solution.py:17
  65.6 85.5 %collective-permute-start.8 = (bf16[1,512,256]{1,2,0:T(8,128)(2,1)}, bf16[1,512,256]{1,2,0:T(8,128)(2,1)S(1)}, u32[]{:S(2)}, u32[]{:S(2)}) collective-permute-start(bf16[1,512,256]{1,2,0:T(8,128)(2,1)} %get-tuple-element.19), channel_id=1, source_target_pairs={{0,1},{2,3},{4,5},{6,7},{8,9},{10,11},{12,13},{14,15},{16,17},{18,... | collective-permute-start | bytes 786440 | tf_op jit(solution)/shard_map/ppermute | solution.py:16
  66.9 84.2 %collective-permute-start.9 = (bf16[1,512,256]{1,2,0:T(8,128)(2,1)}, bf16[1,512,256]{1,2,0:T(8,128)(2,1)}, u32[]{:S(2)}, u32[]{:S(2)}) collective-permute-start(bf16[1,512,256]{1,2,0:T(8,128)(2,1)} %get-tuple-element.20), channel_id=1, source_target_pairs={{1,0},{3,2},{5,4},{7,6},{9,8},{11,10},{13,12},{15,14},{17,16},{19,... | collective-permute-start | bytes 786440 | tf_op jit(solution)/shard_map/ppermute | solution.py:17
  71.9 12.9 %collective-permute-start.2 = (bf16[16,2,30]{2,0,1:T(8,128)(2,1)S(1)}, bf16[16,2,30]{2,0,1:T(8,128)(2,1)S(1)}, u32[]{:S(2)}, u32[]{:S(2)}) collective-permute-start(bf16[16,2,30]{2,0,1:T(8,128)(2,1)S(1)} %get-tuple-element.27), channel_id=1, source_target_pairs={{0,2},{2,4},{4,6},{1,3},{3,5},{5,7},{8,10},{10,12},{12,14},{9,11},... | collective-permute-start | bytes 5768 | tf_op jit(solution)/shard_map/ppermute | solution.py:16
  73.2 13.5 %collective-permute-start.3 = (bf16[16,2,30]{2,0,1:T(8,128)(2,1)S(1)}, bf16[16,2,30]{2,0,1:T(8,128)(2,1)S(1)}, u32[]{:S(2)}, u32[]{:S(2)}) collective-permute-start(bf16[16,2,30]{2,0,1:T(8,128)(2,1)S(1)} %get-tuple-element.28), channel_id=1, source_target_pairs={{2,0},{4,2},{6,4},{3,1},{5,3},{7,5},{10,8},{12,10},{14,12},{11,9},... | collective-permute-start | bytes 5768 | tf_op jit(solution)/shard_map/ppermute | solution.py:17
  79.4 25.9 %collective-permute-start.4 = (bf16[16,2,30]{2,0,1:T(8,128)(2,1)}, bf16[16,2,30]{2,0,1:T(8,128)(2,1)}, u32[]{:S(2)}, u32[]{:S(2)}) collective-permute-start(bf16[16,2,30]{2,0,1:T(8,128)(2,1)} %get-tuple-element.21), channel_id=1, source_target_pairs={{0,8},{8,16},{16,24},{1,9},{9,17},{17,25},{2,10},{10,18},{18,26},{... | collective-permute-start | bytes 5768 | tf_op jit(solution)/shard_map/ppermute | solution.py:16
  84.8 20.5 %collective-permute-start.5 = (bf16[16,2,30]{2,0,1:T(8,128)(2,1)}, bf16[16,2,30]{2,0,1:T(8,128)(2,1)}, u32[]{:S(2)}, u32[]{:S(2)}) collective-permute-start(bf16[16,2,30]{2,0,1:T(8,128)(2,1)} %get-tuple-element.22), channel_id=1, source_target_pairs={{8,0},{16,8},{24,16},{9,1},{17,9},{25,17},{10,2},{18,10},{26,18},{... | collective-permute-start | bytes 5768 | tf_op jit(solution)/shard_map/ppermute | solution.py:17
  87.5 19.4 %copy-start.2 = (f32[16,2,572]{2,0,1:T(8,128)S(1)}, f32[16,2,572]{2,0,1:T(8,128)}, u32[]{:S(2)}) copy-start(f32[16,2,572]{2,0,1:T(8,128)} %all-reduce.14.cloned.1.call-done) | copy-start | bytes 219652
  107.9 8.4 %collective-permute-start.6 = (bf16[16,2,30]{2,0,1:T(8,128)(2,1)S(1)}, bf16[16,2,30]{2,0,1:T(8,128)(2,1)S(1)}, u32[]{:S(2)}, u32[]{:S(2)}) collective-permute-start(bf16[16,2,30]{2,0,1:T(8,128)(2,1)S(1)} %get-tuple-element.23), channel_id=1, source_target_pairs={{0,8},{8,16},{16,24},{1,9},{9,17},{17,25},{2,10},{10,18},{18,26},{... | collective-permute-start | bytes 5768 | tf_op jit(solution)/shard_map/ppermute | solution.py:16
  111.6 5.0 %collective-permute-start.7 = (bf16[16,2,30]{2,0,1:T(8,128)(2,1)S(1)}, bf16[16,2,30]{2,0,1:T(8,128)(2,1)S(1)}, u32[]{:S(2)}, u32[]{:S(2)}) collective-permute-start(bf16[16,2,30]{2,0,1:T(8,128)(2,1)S(1)} %get-tuple-element.24), channel_id=1, source_target_pairs={{8,0},{16,8},{24,16},{9,1},{17,9},{25,17},{10,2},{18,10},{26,18},{... | collective-permute-start | bytes 5768 | tf_op jit(solution)/shard_map/ppermute | solution.py:17
  144.9 7.3 %copy-start.1 = (f32[2,512,256]{1,2,0:T(8,128)S(1)}, f32[2,512,256]{1,2,0:T(8,128)}, u32[]{:S(2)}) copy-start(f32[2,512,256]{1,2,0:T(8,128)} %fusion.1) | copy-start | bytes 3145732
  144.9 7.3 %copy-start.4 = (s32[16,256]{1,0:T(8,128)S(1)}, s32[16,256]{1,0:T(8,128)}, u32[]{:S(2)}) copy-start(s32[16,256]{1,0:T(8,128)} %copy-done.3) | copy-start | bytes 49156
  144.9 7.4 %copy-start.8 = (bf16[16,256]{1,0:T(8,128)(2,1)S(1)}, bf16[16,256]{1,0:T(8,128)(2,1)}, u32[]{:S(2)}) copy-start(bf16[16,256]{1,0:T(8,128)(2,1)} %copy-done.7) | copy-start | bytes 24580
  144.9 7.4 %copy-start.10 = (bf16[16,256]{1,0:T(8,128)(2,1)S(1)}, bf16[16,256]{1,0:T(8,128)(2,1)}, u32[]{:S(2)}) copy-start(bf16[16,256]{1,0:T(8,128)(2,1)} %copy-done.9) | copy-start | bytes 24580
Sparse Core Ops, SparseCore 0:
  34.9 32.1 all-reduce.13
where the time goes:
time: 162 us; the launch traced here: 161 us
  local copies, waits for them, and re-layouts  95.2 us (59%)
  starting transfers between devices  29.4 us (18%)
  between operations  14.6 us (9%)
  blocking collectives  10.7 us (7%)
  other arithmetic  6.41 us (4%)
  matrix products  4.25 us (3%)
    gather x4, local copies, waits for them, and re-layouts, spread(): lax.dynamic_slice_in_dim(skewed, leading - lowest + pad_cells, number, 2)  31.7 us
    reshape x2, local copies, waits for them, and re-layouts, spread(): repeated[:, :shift_levels * (row_length - 1)]  19.1 us
    gather x4, local copies, waits for them, and re-layouts, shear_sum(): lax.dynamic_slice_in_dim(skewed, leading + lowest + pad_cells, number, 1)  18.2 us
    ppermute x5, starting transfers between devices, padded_2(): after = lax.ppermute(leading, axis, down)  16.5 us
    ppermute x5, starting transfers between devices, padded_2(): before = lax.ppermute(last, axis, up)  12.9 us
    psum x1, blocking collectives, on_device(): total_x = lax.psum(summands_x, 'gx')  10.7 us
    reduce_sum x2, local copies, waits for them, and re-layouts, shear_sum(): jnp.sum(flattened.reshape(planes, shift_levels, row_length + 1), axis=1)  8.24 us
    unnamed x36, local copies, waits for them, and re-layouts  3.77 us
  transfers between devices with their start and end apart: 11, of which 1 were waited for; matrix products, arithmetic and copies ran while one was open for 47% of the time, Pallas kernels for 0%

commit v1 on v0

v1 whole, which is shorter than its diff:
```python
import functools

import jax
import jax.numpy as jnp
from jax import lax
from jax.experimental import pallas as pl
from jax.experimental.pallas import tpu as pltpu
from jax.sharding import PartitionSpec as P

SHEAR = 14
LEVELS = SHEAR + 2
VIEWS = 16
TILE = 128
MESH = pl.DeviceIdType.MESH


def slope_rows(slopes_ref, family):
    rows = lax.broadcasted_iota(jnp.int32, (VIEWS, TILE), 0)
    slopes = jnp.zeros((VIEWS, TILE), jnp.int32)
    for view in range(VIEWS):
        slopes = jnp.where(rows == view, slopes_ref[family, view], slopes)
    return slopes


def wide(tile, width):
    return jnp.concatenate([tile] * (width // TILE), axis=1)


def fill_table(table_ref, slopes, cells):
    position = lax.broadcasted_iota(jnp.int32, (VIEWS, cells), 1)
    slope = wide(slopes, cells)
    place = (slope * position - cells * jnp.minimum(slope, 0)).astype(jnp.float32) * (1.0 / cells)
    for level in range(LEVELS):
        weight = jnp.maximum(1.0 - jnp.abs(place - float(level)), 0.0)
        table_ref[level * VIEWS : (level + 1) * VIEWS, :] = weight.astype(jnp.bfloat16)


def leftward(value, amount):
    width = value.shape[1]
    return value if amount % width == 0 else pltpu.roll(value, (width - amount) % width, 1)


def shear_sum(summands, cells, fixed, amount, bits):
    ring = cells + TILE
    blank = jnp.zeros((VIEWS, TILE), jnp.float32)
    parts = [
        jnp.concatenate([summands[s * VIEWS : (s + 1) * VIEWS, :], blank], axis=1)
        for s in range(LEVELS)
    ]
    step = 1
    while len(parts) > 1:
        parts = [a + leftward(b, step) for a, b in zip(parts[::2], parts[1::2])]
        step *= 2
    around = leftward(parts[0], fixed)
    line = jnp.concatenate([around[:, cells:], around[:, :cells], blank], axis=1)
    amounts = wide(amount, cells + 2 * TILE)
    for bit in range(bits):
        chosen = (amounts & (1 << bit)) != 0
        line = jnp.where(chosen, pltpu.roll(line, 1 << bit, 1), line)
    return line


def spread(bins, cells, fixed, amount, bits, out_ref):
    amounts = wide(amount, cells + 2 * TILE)
    for bit in range(bits):
        chosen = (amounts & (1 << bit)) != 0
        bins = jnp.where(chosen, leftward(bins, 1 << bit), bins)
    bins = bins[:, : cells + TILE]
    for level in range(LEVELS):
        moved = pltpu.roll(bins, level + fixed, 1)[:, TILE:]
        out_ref[level * VIEWS : (level + 1) * VIEWS, :] = moved.astype(jnp.bfloat16)


class Family:
    def __init__(self, along, across, n_along, n_across, cells_along, cells, index, refs):
        self.along, self.across = along, across
        self.n, self.m = n_along, n_across
        self.cells_along, self.cells = cells_along, cells
        self.index = index
        self.me, self.place = lax.axis_index(along), lax.axis_index(across)
        self.fixed = SHEAR * (n_along // 2 - 1)
        self.bits = (SHEAR * (n_along - 1)).bit_length()
        self.scale = float(cells_along * n_along) ** -0.5
        (self.table, self.part, self.own, self.left, self.right, self.res, self.spread,
         self.send_sem, self.recv_sem) = refs

    def prepare(self, slopes_ref):
        slopes = slope_rows(slopes_ref, self.index)
        self.amount = self.fixed - slopes * (self.me - self.n // 2) - jnp.minimum(slopes, 0)
        fill_table(self.table, slopes, self.cells_along)

    def forward(self, volume_ref, measured_ref):
        planes = volume_ref.shape[0]
        chunk = self.part.shape[1]
        per = VIEWS // chunk
        for p in range(planes):
            dims = ((1,), (0,)) if self.index == 0 else ((1,), (1,))
            summands = lax.dot_general(
                self.table[...], volume_ref[p], (dims, ((), ())), preferred_element_type=jnp.float32
            )
            line = shear_sum(summands, self.cells, self.fixed, self.amount, self.bits) * self.scale
            measured = measured_ref[:, p, :]
            for c in range(per):
                slot = p * per + c
                piece = line[c * chunk : (c + 1) * chunk]
                mine = jnp.where(self.me == slot, measured[c * chunk : (c + 1) * chunk], 0.0)
                self.part[slot, :, :TILE] = piece[:, :TILE]
                self.part[slot, :, TILE : TILE + self.cells] = piece[:, TILE : TILE + self.cells] - mine
                self.part[slot, :, TILE + self.cells :] = piece[:, TILE + self.cells :]

    def copy(self, src, dst, kind, device):
        return pltpu.make_async_remote_copy(
            src_ref=src, dst_ref=dst, send_sem=self.send_sem.at[kind], recv_sem=self.recv_sem.at[kind],
            device_id=device, device_id_type=MESH,
        )

    def scatter(self):
        cells = self.cells
        for d in range(1, self.n):
            to = lax.rem(self.me + d, self.n)
            self.copy(self.part.at[to], self.own.at[d - 1], 0, {self.along: to}).start()

        @pl.when(self.place < self.m - 1)
        def _():
            for d in range(self.n):
                to = lax.rem(self.me + d, self.n)
                self.copy(
                    self.part.at[to, :, pl.ds(cells, 2 * TILE)], self.left.at[d], 1,
                    {self.along: to, self.across: self.place + 1},
                ).start()

        @pl.when(self.place > 0)
        def _():
            for d in range(self.n):
                to = lax.rem(self.me + d, self.n)
                self.copy(
                    self.part.at[to, :, pl.ds(0, 2 * TILE)], self.right.at[d], 2,
                    {self.along: to, self.across: self.place - 1},
                ).start()

    def nobody(self):
        return {self.along: lax.rem(self.me + 1, self.n)}

    def gather(self):
        cells = self.cells
        self.copy(self.own, self.own, 0, self.nobody()).wait_recv()
        self.res[self.me] = self.part[self.me] + functools.reduce(
            lambda a, b: a + b, [self.own[d] for d in range(self.n - 1)]
        )

        @pl.when(self.place > 0)
        def _():
            self.copy(self.left, self.left, 1, self.nobody()).wait_recv()
            total = functools.reduce(lambda a, b: a + b, [self.left[d] for d in range(self.n)])
            self.res[self.me, :, : 2 * TILE] += total

        @pl.when(self.place < self.m - 1)
        def _():
            self.copy(self.right, self.right, 2, self.nobody()).wait_recv()
            total = functools.reduce(lambda a, b: a + b, [self.right[d] for d in range(self.n)])
            self.res[self.me, :, cells : cells + 2 * TILE] += total

        for d in range(1, self.n):
            to = lax.rem(self.me + d, self.n)
            self.copy(self.res.at[self.me], self.res.at[self.me], 3, {self.along: to}).start()

    def backward(self, out_ref):
        cells = self.cells
        chunk = self.part.shape[1]
        per = VIEWS // chunk
        rest = self.res.at[pl.ds(0, self.n - 1)]
        self.copy(rest, rest, 3, self.nobody()).wait_recv()
        lane = lax.broadcasted_iota(jnp.int32, (VIEWS, cells + 2 * TILE), 1)
        first = jnp.where(self.place == 0, TILE, 0)
        end = jnp.where(self.place == self.m - 1, TILE + cells, cells + 2 * TILE)
        inside = (lane >= first) & (lane < end)
        for p in range(out_ref.shape[1]):
            bins = jnp.concatenate([self.res[p * per + c] for c in range(per)], axis=0)
            out_ref[:, p, :] = bins[:, TILE : TILE + cells]
            bins = jnp.where(inside, bins, 0.0)
            spread(bins, cells, self.fixed, self.amount, self.bits, self.spread.at[p])

    def finish(self):
        self.copy(self.own, self.own, 0, self.nobody()).wait_send()

        @pl.when(self.place < self.m - 1)
        def _():
            self.copy(self.left, self.left, 1, self.nobody()).wait_send()

        @pl.when(self.place > 0)
        def _():
            self.copy(self.right, self.right, 2, self.nobody()).wait_send()

        rest = self.res.at[pl.ds(0, self.n - 1)]
        self.copy(rest, rest, 3, self.nobody()).wait_send()


def kernel(sizes, volume, slopes, measured_x, measured_y, gradient, residual_x, residual_y, *scratch):
    nx, ny, npa = sizes
    planes, cells_x, cells_y = volume.shape
    fx = Family("gx", "gy", nx, ny, cells_x, cells_y, 0, scratch[0:9])
    fy = Family("gy", "gx", ny, nx, cells_y, cells_x, 1, scratch[9:18])
    before, after, plane_send, plane_recv = scratch[18:]
    i, j, k = lax.axis_index("gx"), lax.axis_index("gy"), lax.axis_index("pa")

    barrier = pltpu.get_barrier_semaphore()
    for di in range(nx):
        for dj in range(ny):
            if di or dj:
                pl.semaphore_signal(
                    barrier, inc=1, device_id_type=MESH,
                    device_id={"gx": lax.rem(i + di, nx), "gy": lax.rem(j + dj, ny)},
                )

    @pl.when(k > 0)
    def _():
        pl.semaphore_signal(barrier, inc=1, device_id={"pa": k - 1}, device_id_type=MESH)

    @pl.when(k < npa - 1)
    def _():
        pl.semaphore_signal(barrier, inc=1, device_id={"pa": k + 1}, device_id_type=MESH)

    fy.prepare(slopes)
    fx.prepare(slopes)
    count = nx * ny - 1 + jnp.where(k > 0, 1, 0) + jnp.where(k < npa - 1, 1, 0)
    pl.semaphore_wait(barrier, count)

    def up():
        return pltpu.make_async_remote_copy(
            src_ref=volume.at[planes - 1], dst_ref=before, send_sem=plane_send.at[0],
            recv_sem=plane_recv.at[0], device_id={"pa": lax.rem(k + 1, npa)}, device_id_type=MESH,
        )

    def down():
        return pltpu.make_async_remote_copy(
            src_ref=volume.at[0], dst_ref=after, send_sem=plane_send.at[1],
            recv_sem=plane_recv.at[1], device_id={"pa": lax.rem(k + npa - 1, npa)}, device_id_type=MESH,
        )

    @pl.when(k < npa - 1)
    def _():
        up().start()

    @pl.when(k > 0)
    def _():
        down().start()

    fy.forward(volume, measured_y)
    fy.scatter()
    fx.forward(volume, measured_x)
    fx.scatter()
    fy.gather()
    fx.gather()
    fy.backward(residual_y)
    tn = (((0,), (0,)), ((), ()))
    for p in range(planes):
        gradient[p] = fy.scale * lax.dot_general(
            fy.spread[p], fy.table[...], tn, preferred_element_type=jnp.float32
        )
    fx.backward(residual_x)

    @pl.when(k > 0)
    def _():
        up().wait_recv()

    @pl.when(k == 0)
    def _():
        before[...] = jnp.zeros_like(before)

    @pl.when(k < npa - 1)
    def _():
        down().wait_recv()

    @pl.when(k == npa - 1)
    def _():
        after[...] = jnp.zeros_like(after)

    for p in range(planes):
        low = (before[...] if p == 0 else volume[p - 1]).astype(jnp.float32)
        high = (after[...] if p == planes - 1 else volume[p + 1]).astype(jnp.float32)
        coupling = 0.02 * (2.0 * volume[p].astype(jnp.float32) - low - high)
        gradient[p] += coupling + fx.scale * lax.dot_general(
            fx.table[...], fx.spread[p], tn, preferred_element_type=jnp.float32
        )

    fy.finish()
    fx.finish()

    @pl.when(k < npa - 1)
    def _():
        up().wait_send()

    @pl.when(k > 0)
    def _():
        down().wait_send()


def family_scratch(n, planes, cells_along, cells):
    rows = planes * VIEWS // n
    return [
        pltpu.VMEM((LEVELS * VIEWS, cells_along), jnp.bfloat16),
        pltpu.VMEM((n, rows, cells + 2 * TILE), jnp.float32),
        pltpu.VMEM((n - 1, rows, cells + 2 * TILE), jnp.float32),
        pltpu.VMEM((n, rows, 2 * TILE), jnp.float32),
        pltpu.VMEM((n, rows, 2 * TILE), jnp.float32),
        pltpu.VMEM((n, rows, cells + 2 * TILE), jnp.float32),
        pltpu.VMEM((planes, LEVELS * VIEWS, cells), jnp.bfloat16),
        pltpu.SemaphoreType.DMA((4,)),
        pltpu.SemaphoreType.DMA((4,)),
    ]


def on_device(sizes, volume, view_slopes, measured_x, measured_y):
    nx, ny, _ = sizes
    planes, cells_x, cells_y = volume.shape
    vmem = pl.BlockSpec(memory_space=pltpu.VMEM)
    return pl.pallas_call(
        functools.partial(kernel, sizes),
        out_shape=(
            jax.ShapeDtypeStruct(volume.shape, jnp.float32),
            jax.ShapeDtypeStruct(measured_x.shape, jnp.float32),
            jax.ShapeDtypeStruct(measured_y.shape, jnp.float32),
        ),
        in_specs=[vmem, pl.BlockSpec(memory_space=pltpu.SMEM), vmem, vmem],
        out_specs=(vmem, vmem, vmem),
        scratch_shapes=[
            *family_scratch(nx, planes, cells_x, cells_y),
            *family_scratch(ny, planes, cells_y, cells_x),
            pltpu.VMEM((cells_x, cells_y), jnp.bfloat16),
            pltpu.VMEM((cells_x, cells_y), jnp.bfloat16),
            pltpu.SemaphoreType.DMA((2,)),
            pltpu.SemaphoreType.DMA((2,)),
        ],
        compiler_params=pltpu.CompilerParams(
            collective_id=0, has_side_effects=True, vmem_limit_bytes=32 * 2**20
        ),
    )(volume, view_slopes, measured_x, measured_y)


def solution(mesh):
    sizes = tuple(mesh.shape[name] for name in ("gx", "gy", "pa"))
    return jax.shard_map(
        functools.partial(on_device, sizes),
        mesh=mesh,
        in_specs=(P("pa", "gx", "gy"), P(), P(None, "pa", "gy"), P(None, "pa", "gx")),
        out_specs=(P("pa", "gx", "gy"), P(None, "pa", "gy"), P(None, "pa", "gx")),
        check_vma=False,
    )
```

time: 162 us -> 25.6 us (0.16)
  the two profiles are of different devices: /device:TPU:27 before, /device:TPU:0 now
where the time goes in v1:
time: 25.6 us; the launch traced here: 25.3 us
  Pallas kernels  19.2 us (75%)
  local copies, waits for them, and re-layouts  5.53 us (22%)
  between operations  0.65 us (3%)
    pallas_call x1, Pallas kernels, on_device(): pl.pallas_call(functools.partial(kernel, sizes), out_shape=(jax.ShapeDtyp...  19.2 us
    unnamed x11, local copies, waits for them, and re-layouts  5.53 us

profile of v1, /device:TPU:0, one launch (start us, length us, event | category | flops | bytes accessed | tf_op | source)
XLA Modules:
  0.0 25.3 jit_solution(9099520737470903281)
XLA Ops:
  0.6 0.0 copy-start
  0.6 1.0 %copy-done = bf16[2,512,256]{2,1,0:T(8,128)(2,1)S(1)} copy-done((bf16[2,512,256]{2,1,0:T(8,128)(2,1)S(1)}, bf16[2,512,256]{2,1,0:T(8,128)(2,1)}, u32[]{:S(2)}) %copy-start) | copy-done | bytes 524312
  1.7 0.0 copy-start.1
  1.7 0.8 %copy-done.1 = f32[16,2,512]{2,1,0:T(2,128)S(1)} copy-done((f32[16,2,512]{2,1,0:T(2,128)S(1)}, f32[16,2,512]{2,1,0:T(2,128)}, u32[]{:S(2)}) %copy-start.1) | copy-done | bytes 65560
  2.5 0.0 copy-start.2
  2.5 0.8 %copy-done.2 = f32[16,2,256]{2,1,0:T(2,128)S(1)} copy-done((f32[16,2,256]{2,1,0:T(2,128)S(1)}, f32[16,2,256]{2,1,0:T(2,128)}, u32[]{:S(2)}) %copy-start.2) | copy-done | bytes 32792
  3.3 0.0 copy-start.3
  3.3 0.7 %copy-done.3 = s32[2,16]{1,0:T(2,128)S(1)} copy-done((s32[2,16]{1,0:T(2,128)S(1)}, s32[2,16]{1,0:T(2,128)}, u32[]{:S(2)}) %copy-start.3) | copy-done | bytes 152
  4.0 19.2 %shard_map.67 = (f32[2,512,256]{2,1,0:T(8,128)S(1)}, f32[16,2,256]{2,1,0:T(2,128)S(1)}, f32[16,2,512]{2,1,0:T(2,128)S(1)}) custom-call(bf16[2,512,256]{2,1,0:T(8,128)(2,1)S(1)} %copy-done, s32[2,16]{1,0:T(2,128)S(1)} %copy-done.3, f32[16,2,256]{2,1,0:T(2,128)S(1)} %copy-done.2, f32[16,2,512]{2,1,0:T(2,128)S(1)} %copy-done.1), custom_call_target="tpu_custom_call" | custom-call | tf_op jit(solution)/shard_map/pallas_call | solution.py:317
  23.1 1.0 %copy.10 = f32[2,512,256]{2,1,0:T(8,128)} copy(f32[2,512,256]{2,1,0:T(8,128)S(1)} %get-tuple-element.6) | data formatting | bytes 2097152
  24.1 0.6 %copy.11 = f32[16,2,256]{2,1,0:T(2,128)} copy(f32[16,2,256]{2,1,0:T(2,128)S(1)} %get-tuple-element.7) | data formatting | bytes 65536
  24.7 0.6 %copy.12 = f32[16,2,512]{2,1,0:T(2,128)} copy(f32[16,2,512]{2,1,0:T(2,128)S(1)} %get-tuple-element.8) | data formatting | bytes 131072
Async XLA Ops:
  0.6 1.0 %copy-start = (bf16[2,512,256]{2,1,0:T(8,128)(2,1)S(1)}, bf16[2,512,256]{2,1,0:T(8,128)(2,1)}, u32[]{:S(2)}) copy-start(bf16[2,512,256]{2,1,0:T(8,128)(2,1)} %volume.1) | copy-start | bytes 1572868
  1.7 0.8 %copy-start.1 = (f32[16,2,512]{2,1,0:T(2,128)S(1)}, f32[16,2,512]{2,1,0:T(2,128)}, u32[]{:S(2)}) copy-start(f32[16,2,512]{2,1,0:T(2,128)} %measured_y.1) | copy-start | bytes 196612
  2.5 0.8 %copy-start.2 = (f32[16,2,256]{2,1,0:T(2,128)S(1)}, f32[16,2,256]{2,1,0:T(2,128)}, u32[]{:S(2)}) copy-start(f32[16,2,256]{2,1,0:T(2,128)} %measured_x.1) | copy-start | bytes 98308
  3.3 0.7 %copy-start.3 = (s32[2,16]{1,0:T(2,128)S(1)}, s32[2,16]{1,0:T(2,128)}, u32[]{:S(2)}) copy-start(s32[2,16]{1,0:T(2,128)} %slopes.1) | copy-start | bytes 388

commit v2 on v1

--- a/solution.py
+++ b/solution.py
@@ -81,7 +81,7 @@
         self.fixed = SHEAR * (n_along // 2 - 1)
         self.bits = (SHEAR * (n_along - 1)).bit_length()
         self.scale = float(cells_along * n_along) ** -0.5
-        (self.table, self.part, self.own, self.left, self.right, self.res, self.spread,
+        (self.table, self.spread, self.part, self.own, self.left, self.right, self.res,
          self.send_sem, self.recv_sem) = refs
 
     def prepare(self, slopes_ref):
@@ -195,13 +195,21 @@
         self.copy(rest, rest, 3, self.nobody()).wait_send()
 
 
-def kernel(sizes, volume, slopes, measured_x, measured_y, gradient, residual_x, residual_y, *scratch):
+def exchange(sizes, volume_hbm, slopes_hbm, measured_x_hbm, measured_y_hbm, residual_x, residual_y,
+             table_x, table_y, spread_x, spread_y, volume, before, after, *scratch):
     nx, ny, npa = sizes
     planes, cells_x, cells_y = volume.shape
-    fx = Family("gx", "gy", nx, ny, cells_x, cells_y, 0, scratch[0:9])
-    fy = Family("gy", "gx", ny, nx, cells_y, cells_x, 1, scratch[9:18])
-    before, after, plane_send, plane_recv = scratch[18:]
+    fx = Family("gx", "gy", nx, ny, cells_x, cells_y, 0, (table_x, spread_x, *scratch[0:7]))
+    fy = Family("gy", "gx", ny, nx, cells_y, cells_x, 1, (table_y, spread_y, *scratch[7:14]))
+    slopes, measured_x, measured_y, plane_send, plane_recv, load_sem = scratch[14:]
     i, j, k = lax.axis_index("gx"), lax.axis_index("gy"), lax.axis_index("pa")
+
+    load_slopes = pltpu.make_async_copy(slopes_hbm, slopes, load_sem.at[0])
+    load_volume = pltpu.make_async_copy(volume_hbm, volume, load_sem.at[1])
+    load_x = pltpu.make_async_copy(measured_x_hbm, measured_x, load_sem.at[2])
+    load_y = pltpu.make_async_copy(measured_y_hbm, measured_y, load_sem.at[3])
+    for load in (load_slopes, load_volume, load_y, load_x):
+        load.start()
 
     barrier = pltpu.get_barrier_semaphore()
     for di in range(nx):
@@ -220,8 +228,10 @@
     def _():
         pl.semaphore_signal(barrier, inc=1, device_id={"pa": k + 1}, device_id_type=MESH)
 
+    load_slopes.wait()
     fy.prepare(slopes)
     fx.prepare(slopes)
+    load_volume.wait()
     count = nx * ny - 1 + jnp.where(k > 0, 1, 0) + jnp.where(k < npa - 1, 1, 0)
     pl.semaphore_wait(barrier, count)
 
@@ -245,18 +255,15 @@
     def _():
         down().start()
 
+    load_y.wait()
     fy.forward(volume, measured_y)
     fy.scatter()
+    load_x.wait()
     fx.forward(volume, measured_x)
     fx.scatter()
     fy.gather()
     fx.gather()
     fy.backward(residual_y)
-    tn = (((0,), (0,)), ((), ()))
-    for p in range(planes):
-        gradient[p] = fy.scale * lax.dot_general(
-            fy.spread[p], fy.table[...], tn, preferred_element_type=jnp.float32
-        )
     fx.backward(residual_x)
 
     @pl.when(k > 0)
@@ -274,14 +281,6 @@
     @pl.when(k == npa - 1)
     def _():
         after[...] = jnp.zeros_like(after)
-
-    for p in range(planes):
-        low = (before[...] if p == 0 else volume[p - 1]).astype(jnp.float32)
-        high = (after[...] if p == planes - 1 else volume[p + 1]).astype(jnp.float32)
-        coupling = 0.02 * (2.0 * volume[p].astype(jnp.float32) - low - high)
-        gradient[p] += coupling + fx.scale * lax.dot_general(
-            fx.table[...], fx.spread[p], tn, preferred_element_type=jnp.float32
-        )
 
     fy.finish()
     fx.finish()
@@ -295,16 +294,43 @@
         down().wait_send()
 
 
-def family_scratch(n, planes, cells_along, cells):
+def combine(scale_x, scale_y, residual_x, residual_y, table_x, table_y, spread_x, spread_y, volume, before, after,
+            gradient_hbm, residual_x_hbm, residual_y_hbm, gradient, sem):
+    planes, cells_x, _ = volume.shape
+    stores = [
+        pltpu.make_async_copy(residual_x, residual_x_hbm, sem.at[0]),
+        pltpu.make_async_copy(residual_y, residual_y_hbm, sem.at[1]),
+    ]
+    for store in stores:
+        store.start()
+    tn = (((0,), (0,)), ((), ()))
+    half = cells_x // 2
+    for p in range(planes):
+        for h in range(2):
+            rows = pl.ds(h * half, half)
+            low = (before[rows] if p == 0 else volume[p - 1, rows]).astype(jnp.float32)
+            high = (after[rows] if p == planes - 1 else volume[p + 1, rows]).astype(jnp.float32)
+            coupling = 0.02 * (2.0 * volume[p, rows].astype(jnp.float32) - low - high)
+            back_x = lax.dot_general(table_x[:, rows], spread_x[p], tn, preferred_element_type=jnp.float32)
+            back_y = lax.dot_general(spread_y[p, :, rows], table_y[...], tn, preferred_element_type=jnp.float32)
+            gradient[p, rows] = scale_x * back_x + scale_y * back_y + coupling
+            store = pltpu.make_async_copy(
+                gradient.at[p, rows], gradient_hbm.at[p, rows], sem.at[2 + 2 * p + h]
+            )
+            store.start()
+            stores.append(store)
+    for store in stores:
+        store.wait()
+
+
+def family_scratch(n, planes, cells):
     rows = planes * VIEWS // n
     return [
-        pltpu.VMEM((LEVELS * VIEWS, cells_along), jnp.bfloat16),
         pltpu.VMEM((n, rows, cells + 2 * TILE), jnp.float32),
         pltpu.VMEM((n - 1, rows, cells + 2 * TILE), jnp.float32),
         pltpu.VMEM((n, rows, 2 * TILE), jnp.float32),
         pltpu.VMEM((n, rows, 2 * TILE), jnp.float32),
         pltpu.VMEM((n, rows, cells + 2 * TILE), jnp.float32),
-        pltpu.VMEM((planes, LEVELS * VIEWS, cells), jnp.bfloat16),
         pltpu.SemaphoreType.DMA((4,)),
         pltpu.SemaphoreType.DMA((4,)),
     ]
@@ -314,27 +340,55 @@
     nx, ny, _ = sizes
     planes, cells_x, cells_y = volume.shape
     vmem = pl.BlockSpec(memory_space=pltpu.VMEM)
-    return pl.pallas_call(
-        functools.partial(kernel, sizes),
+    hbm = pl.BlockSpec(memory_space=pltpu.HBM)
+    shape = jax.ShapeDtypeStruct
+    rows = LEVELS * VIEWS
+    held = pl.pallas_call(
+        functools.partial(exchange, sizes),
         out_shape=(
-            jax.ShapeDtypeStruct(volume.shape, jnp.float32),
-            jax.ShapeDtypeStruct(measured_x.shape, jnp.float32),
-            jax.ShapeDtypeStruct(measured_y.shape, jnp.float32),
+            shape(measured_x.shape, jnp.float32),
+            shape(measured_y.shape, jnp.float32),
+            shape((rows, cells_x), jnp.bfloat16),
+            shape((rows, cells_y), jnp.bfloat16),
+            shape((planes, rows, cells_y), jnp.bfloat16),
+            shape((planes, rows, cells_x), jnp.bfloat16),
+            shape(volume.shape, jnp.bfloat16),
+            shape((cells_x, cells_y), jnp.bfloat16),
+            shape((cells_x, cells_y), jnp.bfloat16),
         ),
-        in_specs=[vmem, pl.BlockSpec(memory_space=pltpu.SMEM), vmem, vmem],
-        out_specs=(vmem, vmem, vmem),
+        in_specs=[hbm] * 4,
+        out_specs=(vmem,) * 9,
         scratch_shapes=[
-            *family_scratch(nx, planes, cells_x, cells_y),
-            *family_scratch(ny, planes, cells_y, cells_x),
-            pltpu.VMEM((cells_x, cells_y), jnp.bfloat16),
-            pltpu.VMEM((cells_x, cells_y), jnp.bfloat16),
+            *family_scratch(nx, planes, cells_y),
+            *family_scratch(ny, planes, cells_x),
+            pltpu.SMEM(view_slopes.shape, jnp.int32),
+            pltpu.VMEM(measured_x.shape, jnp.float32),
+            pltpu.VMEM(measured_y.shape, jnp.float32),
             pltpu.SemaphoreType.DMA((2,)),
             pltpu.SemaphoreType.DMA((2,)),
+            pltpu.SemaphoreType.DMA((4,)),
         ],
         compiler_params=pltpu.CompilerParams(
-            collective_id=0, has_side_effects=True, vmem_limit_bytes=32 * 2**20
+            collective_id=0, has_side_effects=True, vmem_limit_bytes=24 * 2**20
         ),
     )(volume, view_slopes, measured_x, measured_y)
+    scale_x = float(cells_x * nx) ** -0.5
+    scale_y = float(cells_y * ny) ** -0.5
+    return pl.pallas_call(
+        functools.partial(combine, scale_x, scale_y),
+        out_shape=(
+            shape(volume.shape, jnp.float32),
+            shape(measured_x.shape, jnp.float32),
+            shape(measured_y.shape, jnp.float32),
+        ),
+        in_specs=[vmem] * 9,
+        out_specs=(hbm,) * 3,
+        scratch_shapes=[
+            pltpu.VMEM(volume.shape, jnp.float32),
+            pltpu.SemaphoreType.DMA((2 + 2 * planes,)),
+        ],
+        compiler_params=pltpu.CompilerParams(vmem_limit_bytes=24 * 2**20),
+    )(*held)
 
 
 def solution(mesh):

time: 25.6 us -> 23.6 us (0.922)
  local copies, waits for them, and re-layouts: 5.53 us -> 3.31 us
    unnamed x11 -> x8, local copies, waits for them, and re-layouts: 5.53 us -> 3.31 us
    pallas_call x1 -> x2, Pallas kernels: 19.2 us -> 19.3 us  [the longest x1 18 us: on_device(): pl.pallas_call(functools.partial(exchange, sizes), out_shape=(shape(measu...]
where the time goes in v2:
time: 23.6 us; the launch traced here: 23.3 us
  Pallas kernels  19.3 us (82%)
  local copies, waits for them, and re-layouts  3.31 us (14%)
  between operations  0.65 us (3%)
    pallas_call x1, Pallas kernels, on_device(): pl.pallas_call(functools.partial(exchange, sizes), out_shape=(shape(measu...  18 us
    unnamed x8, local copies, waits for them, and re-layouts  3.31 us
    pallas_call x1, Pallas kernels, on_device(): pl.pallas_call(functools.partial(combine, scale_x, scale_y), out_shape=(s...  1.34 us

profile of v2, /device:TPU:0, one launch (start us, length us, event | category | flops | bytes accessed | tf_op | source)
XLA Modules:
  0.0 23.3 jit_solution(11807638728216882760)
XLA Ops:
  0.6 0.0 copy-start
  0.6 1.0 %copy-done = bf16[2,512,256]{2,1,0:T(8,128)(2,1)S(1)} copy-done((bf16[2,512,256]{2,1,0:T(8,128)(2,1)S(1)}, bf16[2,512,256]{2,1,0:T(8,128)(2,1)}, u32[]{:S(2)}) %copy-start) | copy-done | bytes 524312
  1.7 0.0 copy-start.1
  1.7 0.8 %copy-done.1 = f32[16,2,512]{2,1,0:T(2,128)S(1)} copy-done((f32[16,2,512]{2,1,0:T(2,128)S(1)}, f32[16,2,512]{2,1,0:T(2,128)}, u32[]{:S(2)}) %copy-start.1) | copy-done | bytes 65560
  2.5 0.0 copy-start.2
  2.5 0.8 %copy-done.2 = f32[16,2,256]{2,1,0:T(2,128)S(1)} copy-done((f32[16,2,256]{2,1,0:T(2,128)S(1)}, f32[16,2,256]{2,1,0:T(2,128)}, u32[]{:S(2)}) %copy-start.2) | copy-done | bytes 32792
  3.3 0.0 copy-start.3
  3.3 0.7 %copy-done.3 = s32[2,16]{1,0:T(2,128)S(1)} copy-done((s32[2,16]{1,0:T(2,128)S(1)}, s32[2,16]{1,0:T(2,128)}, u32[]{:S(2)}) %copy-start.3) | copy-done | bytes 152
  4.0 18.0 %shard_map.67 = (f32[16,2,256]{2,1,0:T(2,128)S(1)}, f32[16,2,512]{2,1,0:T(2,128)S(1)}, bf16[256,512]{1,0:T(8,128)(2,1)S(1)}, bf16[256,256]{1,0:T(8,128)(2,1)S(1)...) custom-call(bf16[2,512,256]{2,1,0:T(8,128)(2,1)S(1)} %copy-done, ...), custom_call_target="tpu_custom_call" | custom-call | tf_op jit(solution)/shard_map/pallas_call | solution.py:346
  22.0 1.3 %shard_map.68 = (f32[2,512,256]{2,1,0:T(8,128)}, f32[16,2,256]{2,1,0:T(2,128)}, f32[16,2,512]{2,1,0:T(2,128)}) custom-call(f32[16,2,256]{2,1,0:T(2,128)S(1)} %get-tuple-element.12.residual_x, f32[16,2,512]{2,1,0:T(2,128)S(1)} %get-tuple-element.13.residual_y, bf16[256,512]{1,0:T(8,128)(2,1)S(1)} %get-tuple-element.14.table_x, ...), custom_call_target="tpu_custom_call" | custom-call | tf_op jit(solution)/shard_map/pallas_call | solution.py:377
Async XLA Ops:
  0.6 1.0 %copy-start = (bf16[2,512,256]{2,1,0:T(8,128)(2,1)S(1)}, bf16[2,512,256]{2,1,0:T(8,128)(2,1)}, u32[]{:S(2)}) copy-start(bf16[2,512,256]{2,1,0:T(8,128)(2,1)} %volume_hbm.1) | copy-start | bytes 1572868
  1.7 0.8 %copy-start.1 = (f32[16,2,512]{2,1,0:T(2,128)S(1)}, f32[16,2,512]{2,1,0:T(2,128)}, u32[]{:S(2)}) copy-start(f32[16,2,512]{2,1,0:T(2,128)} %measured_y_hbm.1) | copy-start | bytes 196612
  2.5 0.8 %copy-start.2 = (f32[16,2,256]{2,1,0:T(2,128)S(1)}, f32[16,2,256]{2,1,0:T(2,128)}, u32[]{:S(2)}) copy-start(f32[16,2,256]{2,1,0:T(2,128)} %measured_x_hbm.1) | copy-start | bytes 98308
  3.3 0.7 %copy-start.3 = (s32[2,16]{1,0:T(2,128)S(1)}, s32[2,16]{1,0:T(2,128)}, u32[]{:S(2)}) copy-start(s32[2,16]{1,0:T(2,128)} %slopes_hbm.1) | copy-start | bytes 388
